TPU v7x, 512 devices: a whole 4x8x8 slice. The times are simulated.
512 devices in a mesh: seq: 64 (over y_lo, x, z), head: 8 (over y_hi, core).
Axes of the slice: x: 4, y: 8 (y_hi: 4, y_lo: 2; y = y_hi * 2 + y_lo), z: 8, core: 2. Of those that a mesh axis runs over, the one named last changes fastest.
Arguments:
- queries: bfloat16 [8192, 3072], P(('seq', 'head')), may hold values from -30 to 30
- key_rows: bfloat16 [8192, 1024], P(('seq', 'head')), may hold values from -30 to 30
- value_rows: bfloat16 [8192, 1024], P(('seq', 'head')), may hold values from -6 to 6
- block_span: int32 [128], replicated, may hold values from 0 to 3, as said below
- attend: int32 [4, 4], replicated, may hold values from 0 to 1, as said below
- noise_level: int32 [4], replicated, may hold values from 0 to 31
- gate_table: float32 [32, 3072], replicated, may hold values from 0.25 to 2
Outputs:
- gated: bfloat16 [8192, 3072], P(('seq', 'head'))
Inputs may be any that keep to these rules, and one draw needn't show every extreme that they name: `block_span`: every span of 0 to 3 owns exactly 32 blocks. attend[r][r] is 1 and attend[r][s] is 0 for s > r.
All inputs are finite; a program needn't handle non-finite values.
Results may differ from a plain program's by a relative error of at most 0.01.
Values may be sent and summed in bfloat16 or wider, within the bound.
A program may use at most 64 MiB of HBM per device.

v0:
```python
import jax
import jax.numpy as jnp
from jax import lax
from jax.sharding import PartitionSpec as P

HD = 128


def span_lookup(token_ids, block_span, block_size):
    block_index = token_ids // block_size
    count_blocks = block_span.shape[0]
    matches = (block_index[:, None] == jnp.arange(count_blocks, dtype=jnp.int32)[None, :]).astype(
        jnp.int32
    )
    return jnp.sum(matches * block_span[None, :], axis=1)


def permitted(query_spans, source_spans, attend):
    count_spans = attend.shape[0]
    labels = jnp.arange(count_spans, dtype=jnp.int32)[None, :]
    query_hot = (query_spans[:, None] == labels).astype(jnp.float32)
    source_hot = (source_spans[:, None] == labels).astype(jnp.float32)
    reader_rows = jnp.dot(query_hot, attend.astype(jnp.float32), precision=lax.Precision.HIGHEST)
    return jnp.dot(reader_rows, source_hot.T, precision=lax.Precision.HIGHEST) > 0.5


def absorb(state_now, group_queries, key_part, value_part, allowed, score_scale):
    count_rows = key_part.shape[0]
    groups_local = group_queries.shape[1]
    key_heads = key_part.reshape(count_rows, groups_local, HD)
    value_heads = value_part.reshape(count_rows, groups_local, HD)
    row_top, row_total, accumulated = state_now
    scores = (
        jnp.einsum("qgrd,kgd->grqk", group_queries, key_heads, preferred_element_type=jnp.float32)
        * score_scale
    )
    masked = jnp.where(allowed[None, None], scores, -1e30)
    new_top = jnp.maximum(row_top, jnp.max(masked, axis=3))
    probs = jnp.where(allowed[None, None], jnp.exp(scores - new_top[..., None]), 0.0)
    new_total = jnp.sum(probs, axis=3)
    summed = jnp.einsum(
        "grqk,kgd->grqd",
        probs.astype(jnp.bfloat16),
        value_heads,
        preferred_element_type=jnp.float32,
    )
    return (new_top, new_total, summed)


def local(queries, key_rows, value_rows, block_span, attend, noise_level, gate_table):
    rows_device = queries.shape[0]
    head_count = lax.axis_size("head")
    tok_group = rows_device * head_count
    block_size = tok_group // 2
    width_local = queries.shape[1] // head_count
    kv_width = key_rows.shape[1] // head_count
    heads_local = width_local // HD
    groups_local = kv_width // HD
    per_group = heads_local // groups_local
    score_scale = HD ** (-0.5)
    seq_index = lax.axis_index("seq")
    head_index = lax.axis_index("head")
    query_ids = seq_index * tok_group + jnp.arange(tok_group, dtype=jnp.int32)
    query_spans = span_lookup(query_ids, block_span, block_size)
    initial = (
        jnp.full((groups_local, per_group, tok_group), -1e30, jnp.float32),
        jnp.zeros((groups_local, per_group, tok_group), jnp.float32),
        jnp.zeros((groups_local, per_group, tok_group, HD), jnp.float32),
    )
    local_q, local_k, local_v = (
        lax.all_to_all(queries, "head", split_axis=1, concat_axis=0, tiled=True),
        lax.all_to_all(key_rows, "head", split_axis=1, concat_axis=0, tiled=True),
        lax.all_to_all(value_rows, "head", split_axis=1, concat_axis=0, tiled=True),
    )
    group_queries = local_q.reshape(tok_group, groups_local, per_group, HD)
    key_part = lax.all_gather(local_k, "seq", axis=0, tiled=True)
    value_part = lax.all_gather(local_v, "seq", axis=0, tiled=True)
    source_ids = jnp.arange(key_part.shape[0], dtype=jnp.int32)
    allowed = permitted(query_spans, span_lookup(source_ids, block_span, block_size), attend)
    final_state = absorb(initial, group_queries, key_part, value_part, allowed, score_scale)
    row_top, row_total, accumulated = final_state
    attn_heads = (accumulated / row_total[..., None]).astype(jnp.bfloat16)
    attn_heads = attn_heads.reshape(heads_local, tok_group, HD)
    attn_local = jnp.transpose(attn_heads, (1, 0, 2)).reshape(tok_group, width_local)
    attn_rows = lax.all_to_all(attn_local, "head", split_axis=0, concat_axis=1, tiled=True)
    own_ids = (seq_index * head_count + head_index) * rows_device + jnp.arange(
        rows_device, dtype=jnp.int32
    )
    own_spans = span_lookup(own_ids, block_span, block_size)
    span_hot = (
        own_spans[:, None] == jnp.arange(noise_level.shape[0], dtype=jnp.int32)[None, :]
    ).astype(jnp.int32)
    own_levels = jnp.sum(span_hot * noise_level[None, :], axis=1)
    level_hot = (
        own_levels[:, None] == jnp.arange(gate_table.shape[0], dtype=jnp.int32)[None, :]
    ).astype(jnp.float32)
    gate_rows = jnp.dot(level_hot, gate_table, precision=lax.Precision.HIGHEST)
    return (gate_rows * attn_rows.astype(jnp.float32)).astype(jnp.bfloat16)


def solution(mesh):
    return jax.shard_map(
        local,
        mesh=mesh,
        in_specs=(
            P(("seq", "head"), None),
            P(("seq", "head"), None),
            P(("seq", "head"), None),
            P(),
            P(),
            P(),
            P(),
        ),
        out_specs=P(("seq", "head"), None),
        check_vma=False,
    )
```

profile of v0, /device:TPU:1, one launch (start us, length us, event | category | flops | bytes accessed | tf_op | source)
XLA Modules:
  0.0 660.6 jit_solution(14707583830658837288)
XLA Ops:
  6.5 0.0 copy-start
  6.5 0.0 all-gather.3.cloned.1.call-start
  6.5 0.8 copy_bitcast_fusion.2
  7.4 17.1 %all_to_all.67 = bf16[16,8,128]{2,0,1:T(8,128)(2,1)} all-to-all(bf16[16,8,128]{2,0,1:T(8,128)(2,1)S(1)} %copy_bitcast_fusion.2), channel_id=1, replica_groups=mesh['seq'=64,'head'=8] {'head'}, dimensions={1} | all-to-all | bytes 65536 | tf_op jit(solution)/shard_map/all_to_all | solution.py:72
  24.5 0.0 all-gather.3.cloned.1.call-update
  24.5 0.0 all-gather.5.cloned.1.call-start
  24.6 0.8 copy_bitcast_fusion.1
  25.3 11.0 %all_to_all.68 = bf16[16,8,128]{2,0,1:T(8,128)(2,1)} all-to-all(bf16[16,8,128]{2,0,1:T(8,128)(2,1)S(1)} %copy_bitcast_fusion.1), channel_id=1, replica_groups=mesh['seq'=64,'head'=8] {'head'}, dimensions={1} | all-to-all | bytes 65536 | tf_op jit(solution)/shard_map/all_to_all | solution.py:73
  36.3 0.0 all-gather.5.cloned.1.call-update
  36.3 1.5 copy.40
  37.9 4.0 all-to-all-start.1
  41.9 0.8 select_reduce_fusion.1
  42.7 3.2 select_reduce_fusion
  45.9 0.9 fusion.31
  46.9 2.2 convolution_compare_fusion
  49.1 2.5 copy.20
  51.6 0.0 all-to-all-done.1
  51.6 0.7 reshape.113
  52.3 229.4 %all-gather.3.cloned.1.call-done = bf16[8192,128]{1,0:T(8,128)(2,1)} async-done(((bf16[128,128]{1,0:T(8,128)(2,1)}), bf16[8192,128]{1,0:T(8,128)(2,1)}) %all-gather.3.cloned.1.call-update) | async-done | bytes 2097168 | tf_op jit(solution)/shard_map/all_gather | solution.py:76
  281.7 4.3 fusion
  286.0 0.0 copy-start.1
  286.0 4.6 copy-done.1
  290.6 3.5 fusion.3
  294.1 291.1 %all-gather.5.cloned.1.call-done = bf16[8192,128]{1,0:T(8,128)(2,1)} async-done(((bf16[128,128]{1,0:T(8,128)(2,1)}), bf16[8192,128]{1,0:T(8,128)(2,1)}) %all-gather.5.cloned.1.call-update) | async-done | bytes 2097168 | tf_op jit(solution)/shard_map/all_gather | solution.py:77
  585.2 0.0 copy-start.2
  585.2 0.0 copy-start.3
  585.2 8.9 %fusion.24 = bf16[128,3,128]{2,0,1:T(8,128)(2,1)S(1)} fusion(bf16[8192,128]{1,0:T(8,128)(2,1)} %all-gather.5.cloned.1.call-done, f32[8192,128,3]{1,0,2:T(8,128)} %copy-done.1, f32[3,128]{1,0:T(4,128)S(1)} %broadcast_maximum_fusion, pred[128,8192]{0,1:T(8,128)(4,1)} %copy.20, f32[128,3]{0,1:T(4,128)S(1)} %bitcast.86), kind=kOutput, calls=%fused_computation.22 | convolution fusion | flops 814841856 | bytes 15830016 | tf_op jit(solution)/shard_map/grqk,kgd->grqd/dot_general | solution.py:41
  594.2 0.1 copy.26
  594.3 0.7 all_to_all.61
  595.0 49.7 %all-to-all-start.3 = ((bf16[8,16,384]{2,1,0:T(8,128)(2,1)}), bf16[8,16,384]{2,1,0:T(8,128)(2,1)S(1)}, u32[]{:S(2)}, u32[]{:S(2)}) async-start(bf16[8,16,384]{2,1,0:T(8,128)(2,1)} %all_to_all.61), calls=%async_computation.3 | async-start | bytes 196608 | tf_op jit(solution)/shard_map/all_to_all | solution.py:85
  644.7 0.0 copy-done.2
  644.7 0.2 select_reduce_fusion.2
  644.9 0.0 copy-done.3
  644.9 0.1 select_reduce_fusion.3
  645.0 7.8 %all-to-all-done.3 = bf16[8,16,384]{2,1,0:T(8,128)(2,1)S(1)} async-done(((bf16[8,16,384]{2,1,0:T(8,128)(2,1)}), bf16[8,16,384]{2,1,0:T(8,128)(2,1)S(1)}, u32[]{:S(2)}, u32[]{:S(2)}) %all-to-all-start.3) | async-done | bytes 98336 | tf_op jit(solution)/shard_map/all_to_all | solution.py:85
  652.8 0.0 copy-done
  652.8 0.9 fusion.11
  (6 shorter events, 0.1 us)
Async XLA Ops:
  6.5 646.2 %copy-start = (f32[32,3072]{1,0:T(8,128)S(1)}, f32[32,3072]{1,0:T(8,128)}, u32[]{:S(2)}) copy-start(f32[32,3072]{1,0:T(8,128)} %param.13) | copy-start | bytes 1179652
  6.5 275.2 %all-gather.3.cloned.1.call-start = ((), (), s32[]{:S(2)}) async-start(), calls=%async_computation.4 | async-start | bytes 2129920 | tf_op jit(solution)/shard_map/all_gather | solution.py:76
  24.5 560.7 %all-gather.5.cloned.1.call-start = ((), (), s32[]{:S(2)}) async-start(), calls=%async_computation.5 | async-start | bytes 2129920 | tf_op jit(solution)/shard_map/all_gather | solution.py:77
  37.9 13.8 %all-to-all-start.1 = ((bf16[16,8,384]{2,0,1:T(8,128)(2,1)}), bf16[16,8,384]{2,0,1:T(8,128)(2,1)S(1)}, u32[]{:S(2)}, u32[]{:S(2)}) async-start(bf16[16,8,384]{2,0,1:T(8,128)(2,1)} %bitcast.80), calls=%async_computation.1 | async-start | bytes 196608 | tf_op jit(solution)/shard_map/all_to_all | solution.py:71
  286.0 4.6 copy-start.1
  585.2 59.5 %copy-start.2 = (s32[128]{0:T(128)S(1)}, s32[128]{0:T(128)}, u32[]{:S(2)}) copy-start(s32[128]{0:T(128)} %param.10) | copy-start | bytes 1540
  585.2 59.6 %copy-start.3 = (s32[4]{0:T(128)S(1)}, s32[4]{0:T(128)}, u32[]{:S(2)}) copy-start(s32[4]{0:T(128)} %param.12) | copy-start | bytes 52
  595.0 57.7 %all-to-all-start.3 = ((bf16[8,16,384]{2,1,0:T(8,128)(2,1)}), bf16[8,16,384]{2,1,0:T(8,128)(2,1)S(1)}, u32[]{:S(2)}, u32[]{:S(2)}) async-start(bf16[8,16,384]{2,1,0:T(8,128)(2,1)} %all_to_all.61), calls=%async_computation.3 | async-start | bytes 196608 | tf_op jit(solution)/shard_map/all_to_all | solution.py:85
Sparse Core Ops, SparseCore 0:
  24.6 257.0 all-gather.2
  283.8 301.4 all-gather.4
where the time goes:
time: 661 us
  waiting for transfers between devices  528 us (80%)
  starting transfers between devices  53.7 us (8%)
  blocking collectives  28.1 us (4%)
  matrix products  17.3 us (3%)
  between operations  13.5 us (2%)
  local copies, waits for them, and re-layouts  11.7 us (2%)
  other arithmetic  7.88 us (1%)
    all_gather x1, waiting for transfers between devices, local(): value_part = lax.all_gather(local_v, 'seq', axis=0, tiled=True)  291 us
    all_gather x1, waiting for transfers between devices, local(): key_part = lax.all_gather(local_k, 'seq', axis=0, tiled=True)  229 us
    all_to_all x1, starting transfers between devices, local(): lax.all_to_all(attn_local, 'head', split_axis=0, concat_axis=1, tiled=True)  49.7 us
    all_to_all x1, blocking collectives, local(): lax.all_to_all(key_rows, 'head', split_axis=1, concat_axis=0, tiled=True)  17.1 us
  transfers between devices with their start and end apart: 4, of which 3 were waited for; matrix products, arithmetic and copies ran while one was open for 3% of the time, Pallas kernels for 0%

commit v1 on v0

v1 whole, which is shorter than its diff:
```python
import functools
import math

import jax
import jax.numpy as jnp
from jax import lax
from jax.experimental import pallas as pl
from jax.experimental.pallas import tpu as pltpu
from jax.sharding import PartitionSpec as P

MESH = pl.DeviceIdType.MESH
HD = 128
NX, NY, NZ = 4, 8, 8
ROWS = 16
HPG = 3
TOK = NY * ROWS
QR = HPG * TOK
COEF = HD**-0.5 * math.log2(math.e)
NEG = -1e30

Y_FAR = (4, 3, 5, 2, 6, 1, 7)
Y_NEAR = (1, 7, 2, 6, 3, 5, 4)
Z_DIRECT = (1, 7, 2, 6, 3, 5)
X_FAR = (2, 1, 3)


def wrap(a, n):
    return lax.rem(a + n, n)


def place():
    seq, head = lax.axis_index("seq"), lax.axis_index("head")
    z, x, y_lo = lax.rem(seq, NZ), lax.rem(seq // NZ, NX), seq // (NZ * NX)
    return x, (head // 2) * 2 + y_lo, z, lax.rem(head, 2)


def device(x, y, z, core):
    return ((lax.rem(y, 2) * NX + x) * NZ + z, (y // 2) * 2 + core)


def block_of(x, y, z):
    return ((lax.rem(y, 2) * NX + x) * NZ + z) * 2 + y // 4


def kernel(
    q_hbm, k_hbm, v_hbm, span_ref, attend_ref, level_ref, gate_hbm, out_ref,
    q_in, k_in, v_in, gate, kv, qs, kaug, qaug, vt, acc, top, o_send, s_send, o_recv, s_recv,
    attn_send, attn, in_sem, ykv_s, ykv_r, yq_s, yq_r, z_s, z_r, z4_s, z4_r, c_s, c_r, xq_s, xq_r,
    xo_s, xo_r, xs_s, xs_r, yo_s, yo_r,
):
    x, y, z, core = place()

    def at_x(d):
        return device(wrap(x + d, NX), y, z, core)

    def at_y(d):
        return device(x, wrap(y + d, NY), z, core)

    def at_z(d):
        return device(x, y, wrap(z + d, NZ), core)

    sibling = device(x, y, z, 1 - core)

    def remote(src, dst, ss, rs, to):
        return pltpu.make_async_remote_copy(
            src_ref=src, dst_ref=dst, send_sem=ss, recv_sem=rs, device_id=to, device_id_type=MESH
        )

    loads = [
        pltpu.make_async_copy(k_hbm, k_in, in_sem.at[0]),
        pltpu.make_async_copy(v_hbm, v_in, in_sem.at[1]),
        pltpu.make_async_copy(q_hbm, q_in, in_sem.at[2]),
        pltpu.make_async_copy(gate_hbm, gate, in_sem.at[3]),
    ]
    for load in loads:
        load.start()
    barrier = pltpu.get_barrier_semaphore()
    peers = [at_y(d) for d in Y_FAR] + [at_z(d) for d in Z_DIRECT] + [at_x(d) for d in X_FAR]
    peers.append(sibling)
    for peer in peers:
        pl.semaphore_signal(barrier, inc=1, device_id=peer, device_id_type=MESH)

    lane = lax.broadcasted_iota(jnp.int32, (ROWS, HD), 1)
    for i in range(NY):
        ys = wrap(y - i, NY)
        for j in range(NZ):
            span = span_ref[block_of(x, ys, wrap(z - j, NZ))]
            kaug[j, i * ROWS : (i + 1) * ROWS, :] = jnp.where(lane == span, 1.0, 0.0).astype(jnp.bfloat16)
        for j in range(NX):
            span = span_ref[block_of(wrap(x - j, NX), ys, z)]
            bias = jnp.zeros((ROWS, HD), jnp.float32)
            for s in range(4):
                low = jnp.where(attend_ref[span, s] > 0, 0.0, NEG)
                bias = jnp.where(lane == s, low, bias)
            qaug[j, i * ROWS : (i + 1) * ROWS, :] = bias.astype(jnp.bfloat16)

    for load in loads:
        load.wait()
    pl.semaphore_wait(barrier, len(peers))

    def group(d):
        return wrap(y + d, NY)

    def columns(first, count):
        return pl.ds(pl.multiple_of(first * HD, HD), count * HD)

    for d in Y_FAR:
        cols = columns(group(d), 1)
        remote(k_in.at[:, cols], kv.at[0, 0, 0, d], ykv_s.at[d], ykv_r.at[d], at_y(d)).start()
        remote(v_in.at[:, cols], kv.at[0, 0, 1, d], ykv_s.at[d], ykv_r.at[d], at_y(d)).start()
    for d in Y_FAR:
        for h in range(HPG):
            remote(
                q_in.at[:, columns(group(d) * HPG + h, 1)], qs.at[0, h, d], yq_s.at[d], yq_r.at[d], at_y(d)
            ).start()
    kv[0, 0, 0, 0] = k_in[:, columns(y, 1)]
    kv[0, 0, 1, 0] = v_in[:, columns(y, 1)]
    for h in range(HPG):
        qs[0, h, 0] = q_in[:, columns(y * HPG + h, 1)]

    def send_kv(i):
        for d in Z_DIRECT:
            remote(kv.at[0, 0, :, i], kv.at[0, d, :, i], z_s.at[d], z_r.at[d], at_z(d)).start()

    def send_q(i):
        for d in X_FAR:
            remote(qs.at[0, :, i], qs.at[d, :, i], xq_s.at[d], xq_r.at[d], at_x(d)).start()

    send_kv(0)
    send_q(0)
    for d in Y_NEAR:
        unit = kv.at[0, 0, :, d]
        remote(unit, unit, ykv_s.at[d], ykv_r.at[d], sibling).wait_recv()
        send_kv(d)
    remote(kv.at[0, 0], kv.at[1, 0], c_s.at[0], c_r.at[0], sibling).start()
    for d in Y_NEAR:
        unit = qs.at[0, :, d]
        remote(unit, unit, yq_s.at[d], yq_r.at[d], sibling).wait_recv()
        send_q(d)

    def arrive(d):
        slot = kv.at[0, d]
        remote(slot, slot, z_s.at[d], z_r.at[d], sibling).wait_recv()
        remote(slot, kv.at[1, d], c_s.at[d], c_r.at[d], sibling).start()

    def from_sibling(d):
        slot = kv.at[1, d]
        remote(slot, slot, c_s.at[d], c_r.at[d], sibling).wait_recv()

    def turn_values(step, parts):
        for n, (p, d) in enumerate(parts):
            vals = kv[p, d, 1].reshape(TOK, HD)
            vt[step, :, n * TOK : (n + 1) * TOK] = vals.astype(jnp.float32).T.astype(jnp.bfloat16)

    def absorb(step, parts, b, first):
        keys = jnp.concatenate([kv[p, d, 0].reshape(TOK, HD) for p, d in parts], axis=0)
        marks = jnp.concatenate([kaug[d] for _, d in parts], axis=0)
        left = jnp.concatenate([keys, marks], axis=1)
        right = jnp.concatenate(
            [qs[b].reshape(QR, HD), jnp.concatenate([qaug[b]] * HPG, axis=0)], axis=1
        )
        scores = lax.dot_general(left, right, (((1,), (1,)), ((), ())), preferred_element_type=jnp.float32)
        high = jnp.max(scores, axis=0, keepdims=True)
        if not first:
            old = top[b]
            high = jnp.maximum(high, old)
        probs = jnp.exp2((scores - high) * COEF).astype(jnp.bfloat16)
        vals = jnp.concatenate([vt[step], jnp.ones((16, 2 * TOK), jnp.bfloat16)], axis=0)
        new = jnp.dot(vals, probs, preferred_element_type=jnp.float32)
        if first:
            acc[b] = new
        else:
            acc[b] = acc[b] * jnp.exp2((old - high) * COEF) + new
        top[b] = high

    steps = [
        ((0, 0), (1, 0)),
        ((0, 1), (0, 7)),
        ((1, 1), (1, 7)),
        ((0, 2), (0, 6)),
        ((1, 2), (1, 6)),
        ((0, 3), (0, 5)),
        ((1, 3), (1, 5)),
        ((0, 4), (1, 4)),
    ]

    from_sibling(0)
    turn_values(0, steps[0])
    absorb(0, steps[0], 0, True)
    arrive(1)
    arrive(7)
    arrive(2)
    arrive(6)
    remote(kv.at[0, 2, 0], kv.at[0, 4, 0], z4_s.at[0], z4_r.at[0], at_z(2)).start()
    remote(kv.at[0, 6, 1], kv.at[0, 4, 1], z4_s.at[1], z4_r.at[1], at_z(6)).start()
    for d in X_FAR:
        block = qs.at[d]
        remote(block, block, xq_s.at[d], xq_r.at[d], sibling).wait_recv()
    for b in (1, 2, 3):
        absorb(0, steps[0], b, True)
    arrive(3)
    arrive(5)
    for step in (1, 2, 3, 4):
        if step in (2, 4):
            for _, d in steps[step]:
                from_sibling(d)
        turn_values(step, steps[step])
        for b in range(NX):
            absorb(step, steps[step], b, False)
        if step == 2:
            for half in (0, 1):
                slot = kv.at[0, 4, half]
                remote(slot, slot, z4_s.at[half], z4_r.at[half], sibling).wait_recv()
            remote(kv.at[0, 4], kv.at[1, 4], c_s.at[4], c_r.at[4], sibling).start()
    from_sibling(3)
    from_sibling(5)
    from_sibling(4)
    for step in (5, 6, 7):
        turn_values(step, steps[step])
    for b in (2, 1, 3, 0):
        for step in (5, 6, 7):
            absorb(step, steps[step], b, False)
        if b:
            o_send[b] = (acc[b, 0:HD, :] / acc[b, HD : HD + 1, :]).astype(jnp.bfloat16)
            s_send[b] = jnp.concatenate([top[b], acc[b, HD : HD + 7, :]], axis=0)
            to = at_x(-b)
            remote(o_send.at[b], o_recv.at[b], xo_s.at[b], xo_r.at[b], to).start()
            remote(s_send.at[b], s_recv.at[b], xs_s.at[b], xs_r.at[b], to).start()

    for b in (1, 2, 3):
        part, stat = o_recv.at[b], s_recv.at[b]
        remote(stat, stat, xs_s.at[b], xs_r.at[b], sibling).wait_recv()
        remote(part, part, xo_s.at[b], xo_r.at[b], sibling).wait_recv()
    tops = [top[0]] + [s_recv[b, 0:1, :] for b in (1, 2, 3)]
    highest = functools.reduce(jnp.maximum, tops)
    scales = [jnp.exp2((t - highest) * COEF) for t in tops]
    sums = [acc[0, HD : HD + 1, :]] + [s_recv[b, 1:2, :] for b in (1, 2, 3)]
    shares = [scale * total for scale, total in zip(scales, sums)]
    whole = 1.0 / functools.reduce(jnp.add, shares)
    merged = acc[0, 0:HD, :] * (scales[0] * whole)
    for b in (1, 2, 3):
        merged = merged + o_recv[b].astype(jnp.float32) * (shares[b] * whole)
    for h in range(HPG):
        rows = merged[:, h * TOK : (h + 1) * TOK].T.astype(jnp.bfloat16)
        for i in range(NY):
            attn_send[i, :, h * HD : (h + 1) * HD] = rows[i * ROWS : (i + 1) * ROWS, :]
    for d in Y_FAR:
        remote(attn_send.at[d], attn.at[y], yo_s.at[d], yo_r.at[d], at_y(-d)).start()
    attn[y] = attn_send[0]
    level = level_ref[span_ref[block_of(x, y, z)]]
    gates = gate[pl.ds(level, 1), :]
    for d in Y_NEAR:
        unit = attn_send.at[d]
        remote(unit, unit, yo_s.at[d], yo_r.at[d], sibling).wait_recv()
    for g in range(NY):
        cols = slice(g * HPG * HD, (g + 1) * HPG * HD)
        out_ref[:, cols] = (gates[:, cols] * attn[g].astype(jnp.float32)).astype(jnp.bfloat16)

    for d in Y_NEAR:
        remote(kv.at[0, 0, :, d], kv.at[0, 0, :, d], ykv_s.at[d], ykv_r.at[d], sibling).wait_send()
        remote(qs.at[0, :, d], qs.at[0, :, d], yq_s.at[d], yq_r.at[d], sibling).wait_send()
        remote(attn_send.at[d], attn_send.at[d], yo_s.at[d], yo_r.at[d], sibling).wait_send()
    for d in Z_DIRECT:
        remote(kv.at[0, 0], kv.at[0, 0], z_s.at[d], z_r.at[d], sibling).wait_send()
    for half in (0, 1):
        remote(kv.at[0, 4, half], kv.at[0, 4, half], z4_s.at[half], z4_r.at[half], sibling).wait_send()
    for d in range(NZ):
        remote(kv.at[0, d], kv.at[0, d], c_s.at[d], c_r.at[d], sibling).wait_send()
    for d in X_FAR:
        remote(qs.at[0], qs.at[0], xq_s.at[d], xq_r.at[d], sibling).wait_send()
        remote(o_send.at[d], o_send.at[d], xo_s.at[d], xo_r.at[d], sibling).wait_send()
        remote(s_send.at[d], s_send.at[d], xs_s.at[d], xs_r.at[d], sibling).wait_send()


def local(queries, key_rows, value_rows, block_span, attend, noise_level, gate_table):
    bf16, f32 = jnp.bfloat16, jnp.float32
    dma = pltpu.SemaphoreType.DMA
    anywhere = pl.BlockSpec(memory_space=pl.ANY)
    smem = pl.BlockSpec(memory_space=pltpu.SMEM)
    return pl.pallas_call(
        kernel,
        out_shape=jax.ShapeDtypeStruct(queries.shape, bf16),
        in_specs=[anywhere, anywhere, anywhere, smem, smem, smem, anywhere],
        out_specs=pl.BlockSpec(memory_space=pltpu.VMEM),
        scratch_shapes=[
            pltpu.VMEM(queries.shape, bf16),
            pltpu.VMEM(key_rows.shape, bf16),
            pltpu.VMEM(value_rows.shape, bf16),
            pltpu.VMEM(gate_table.shape, f32),
            pltpu.VMEM((2, NZ, 2, NY, ROWS, HD), bf16),
            pltpu.VMEM((NX, HPG, NY, ROWS, HD), bf16),
            pltpu.VMEM((NZ, TOK, HD), bf16),
            pltpu.VMEM((NX, TOK, HD), bf16),
            pltpu.VMEM((8, HD, 2 * TOK), bf16),
            pltpu.VMEM((NX, HD + 16, QR), f32),
            pltpu.VMEM((NX, 1, QR), f32),
            pltpu.VMEM((NX, HD, QR), bf16),
            pltpu.VMEM((NX, 8, QR), f32),
            pltpu.VMEM((NX, HD, QR), bf16),
            pltpu.VMEM((NX, 8, QR), f32),
            pltpu.VMEM((NY, ROWS, HPG * HD), bf16),
            pltpu.VMEM((NY, ROWS, HPG * HD), bf16),
            dma((4,)),
            dma((8,)), dma((8,)), dma((8,)), dma((8,)),
            dma((8,)), dma((8,)), dma((2,)), dma((2,)),
            dma((8,)), dma((8,)),
            dma((4,)), dma((4,)), dma((4,)), dma((4,)), dma((4,)), dma((4,)),
            dma((8,)), dma((8,)),
        ],
        compiler_params=pltpu.CompilerParams(
            collective_id=0, has_side_effects=True, vmem_limit_bytes=48 << 20
        ),
    )(queries, key_rows, value_rows, block_span, attend, noise_level, gate_table)


def solution(mesh):
    rows = P(("seq", "head"), None)
    return jax.shard_map(
        local,
        mesh=mesh,
        in_specs=(rows, rows, rows, P(), P(), P(), P()),
        out_specs=rows,
        check_vma=False,
    )
```

time: 661 us -> 54.5 us (0.08)
  waiting for transfers between devices: 528 us -> 0 us
  starting transfers between devices: 53.7 us -> 0 us
  Pallas kernels: 0 us -> 47.9 us
  blocking collectives: 28.1 us -> 0 us
  matrix products: 17.3 us -> 0 us
  between operations: 13.5 us -> 0.02 us
  other arithmetic: 7.88 us -> 0 us
    all_gather x2 -> x0, waiting for transfers between devices: 521 us -> none  [the longest x1 291 us: local(): value_part = lax.all_gather(local_v, 'seq', axis=0, tiled=True)]
    all_to_all x2 -> x0, starting transfers between devices: 53.7 us -> none  [the longest x1 49.7 us: local(): lax.all_to_all(attn_local, 'head', split_axis=0, concat_axis=1, tiled=True)]
    pallas_call x0 -> x1, Pallas kernels: none -> 47.9 us  [local(): pl.pallas_call(kernel, out_shape=jax.ShapeDtypeStruct(queries.shape, bf16...]
    all_to_all x2 -> x0, blocking collectives: 28.1 us -> none  [the longest x1 17.1 us: local(): lax.all_to_all(key_rows, 'head', split_axis=1, concat_axis=0, tiled=True)]
    dot_general x5 -> x0, matrix products: 17.3 us -> none  [the longest x1 8.93 us: absorb(): jnp.einsum('grqk,kgd->grqd', probs.astype(jnp.bfloat16), value_heads, pre...]
    reduce_sum x5 -> x0, other arithmetic: 7.84 us -> none  [the longest x3 4.22 us: span_lookup(): return jnp.sum(matches * block_span[None, :], axis=1)]
    all_to_all x2 -> x0, waiting for transfers between devices: 7.77 us -> none  [the longest x1 7.77 us: local(): lax.all_to_all(attn_local, 'head', split_axis=0, concat_axis=1, tiled=True)]
  transfers between devices with their start and end apart: 4 -> 0, of which waited for: 3 -> 0; matrix products, arithmetic and copies ran while one was open for 3% -> 0% of each run, Pallas kernels for 0% -> 0%
where the time goes in v1:
time: 54.5 us; the launch traced here: 54 us
  Pallas kernels  47.9 us (88%)
  local copies, waits for them, and re-layouts  6.04 us (11%)
    pallas_call x1, Pallas kernels, local(): pl.pallas_call(kernel, out_shape=jax.ShapeDtypeStruct(queries.shape, bf16...  47.9 us
    unnamed x15, local copies, waits for them, and re-layouts  6.04 us

profile of v1, /device:TPU:1, one launch (start us, length us, event | category | flops | bytes accessed | tf_op | source)
XLA Modules:
  0.0 54.0 jit_solution(8324829093890123394)
XLA Ops:
  0.0 0.0 copy-start
  0.0 1.0 %copy-done = f32[32,3072]{1,0:T(8,128)S(1)} copy-done((f32[32,3072]{1,0:T(8,128)S(1)}, f32[32,3072]{1,0:T(8,128)}, u32[]{:S(2)}) %copy-start) | copy-done | bytes 393240
  1.0 0.0 copy-start.1
  1.0 0.9 %copy-done.1 = bf16[16,3072]{1,0:T(8,128)(2,1)S(1)} copy-done((bf16[16,3072]{1,0:T(8,128)(2,1)S(1)}, bf16[16,3072]{1,0:T(8,128)(2,1)}, u32[]{:S(2)}) %copy-start.1) | copy-done | bytes 98328
  1.9 0.0 copy-start.2
  1.9 0.8 %copy-done.2 = bf16[16,1024]{1,0:T(8,128)(2,1)S(1)} copy-done((bf16[16,1024]{1,0:T(8,128)(2,1)S(1)}, bf16[16,1024]{1,0:T(8,128)(2,1)}, u32[]{:S(2)}) %copy-start.2) | copy-done | bytes 32792
  2.6 0.0 copy-start.3
  2.7 0.8 %copy-done.3 = bf16[16,1024]{1,0:T(8,128)(2,1)S(1)} copy-done((bf16[16,1024]{1,0:T(8,128)(2,1)S(1)}, bf16[16,1024]{1,0:T(8,128)(2,1)}, u32[]{:S(2)}) %copy-start.3) | copy-done | bytes 32792
  3.4 0.0 copy-start.4
  3.4 0.7 %copy-done.4 = s32[4,4]{1,0:T(4,128)S(1)} copy-done((s32[4,4]{1,0:T(4,128)S(1)}, s32[4,4]{1,0:T(4,128)}, u32[]{:S(2)}) %copy-start.4) | copy-done | bytes 88
  4.1 0.0 copy-start.5
  4.1 0.7 %copy-done.5 = s32[128]{0:T(128)S(1)} copy-done((s32[128]{0:T(128)S(1)}, s32[128]{0:T(128)}, u32[]{:S(2)}) %copy-start.5) | copy-done | bytes 536
  4.7 0.0 copy-start.6
  4.7 0.7 %copy-done.6 = s32[4]{0:T(128)S(1)} copy-done((s32[4]{0:T(128)S(1)}, s32[4]{0:T(128)}, u32[]{:S(2)}) %copy-start.6) | copy-done | bytes 40
  5.4 47.9 %shard_map.73 = bf16[16,3072]{1,0:T(8,128)(2,1)S(1)} custom-call(bf16[16,3072]{1,0:T(8,128)(2,1)S(1)} %copy-done.1, bf16[16,1024]{1,0:T(8,128)(2,1)S(1)} %copy-done.2, bf16[16,1024]{1,0:T(8,128)(2,1)S(1)} %copy-done.3, s32[128]{0:T(128)S(1)} %copy-done.5, s32[4,4]{1,0:T(4,128)S(1)} %copy-done.4, s32[4]{0:T(128)S(1)} %copy-done.6, f32[32,3072]{1,0:T(8,128)S(1)} %copy-done), custom_call_target="tpu_custom_call" | custom-call | tf_op jit(solution)/shard_map/pallas_call | solution.py:280
  53.3 0.6 %copy.9 = bf16[16,3072]{1,0:T(8,128)(2,1)} copy(bf16[16,3072]{1,0:T(8,128)(2,1)S(1)} %shard_map.73) | data formatting | bytes 196608
Async XLA Ops:
  0.0 1.0 %copy-start = (f32[32,3072]{1,0:T(8,128)S(1)}, f32[32,3072]{1,0:T(8,128)}, u32[]{:S(2)}) copy-start(f32[32,3072]{1,0:T(8,128)} %gate_hbm.1) | copy-start | bytes 1179652
  1.0 0.9 %copy-start.1 = (bf16[16,3072]{1,0:T(8,128)(2,1)S(1)}, bf16[16,3072]{1,0:T(8,128)(2,1)}, u32[]{:S(2)}) copy-start(bf16[16,3072]{1,0:T(8,128)(2,1)} %q_hbm.1) | copy-start | bytes 294916
  1.9 0.8 %copy-start.2 = (bf16[16,1024]{1,0:T(8,128)(2,1)S(1)}, bf16[16,1024]{1,0:T(8,128)(2,1)}, u32[]{:S(2)}) copy-start(bf16[16,1024]{1,0:T(8,128)(2,1)} %k_hbm.1) | copy-start | bytes 98308
  2.6 0.8 %copy-start.3 = (bf16[16,1024]{1,0:T(8,128)(2,1)S(1)}, bf16[16,1024]{1,0:T(8,128)(2,1)}, u32[]{:S(2)}) copy-start(bf16[16,1024]{1,0:T(8,128)(2,1)} %v_hbm.1) | copy-start | bytes 98308
  3.4 0.7 %copy-start.4 = (s32[4,4]{1,0:T(4,128)S(1)}, s32[4,4]{1,0:T(4,128)}, u32[]{:S(2)}) copy-start(s32[4,4]{1,0:T(4,128)} %attend_ref.1) | copy-start | bytes 196
  4.1 0.7 %copy-start.5 = (s32[128]{0:T(128)S(1)}, s32[128]{0:T(128)}, u32[]{:S(2)}) copy-start(s32[128]{0:T(128)} %span_ref.1) | copy-start | bytes 1540
  4.7 0.7 %copy-start.6 = (s32[4]{0:T(128)S(1)}, s32[4]{0:T(128)}, u32[]{:S(2)}) copy-start(s32[4]{0:T(128)} %level_ref.1) | copy-start | bytes 52

commit v2 on v1

--- a/solution.py
+++ b/solution.py
@@ -20,7 +20,7 @@
 
 Y_FAR = (4, 3, 5, 2, 6, 1, 7)
 Y_NEAR = (1, 7, 2, 6, 3, 5, 4)
-Z_DIRECT = (1, 7, 2, 6, 3, 5)
+Z_DIRECT = (2, 6, 1, 7)
 X_FAR = (2, 1, 3)
 
 
@@ -43,9 +43,9 @@
 
 
 def kernel(
-    q_hbm, k_hbm, v_hbm, span_ref, attend_ref, level_ref, gate_hbm, out_ref,
-    q_in, k_in, v_in, gate, kv, qs, kaug, qaug, vt, acc, top, o_send, s_send, o_recv, s_recv,
-    attn_send, attn, in_sem, ykv_s, ykv_r, yq_s, yq_r, z_s, z_r, z4_s, z4_r, c_s, c_r, xq_s, xq_r,
+    q_hbm, k_hbm, v_hbm, span_hbm, attend_hbm, level_hbm, gate_hbm, out_ref,
+    q_in, k_in, v_in, gate, span_ref, attend_ref, level_ref, kv, qs, kaug, qaug, vt, acc, top, o_send, s_send, o_recv, s_recv,
+    attn_send, attn, in_sem, ykv_s, ykv_r, yq_s, yq_r, z_s, z_r, zu_r, z4_s, z4_r, c_s, c_r, xq_s, xq_r,
     xo_s, xo_r, xs_s, xs_r, yo_s, yo_r,
 ):
     x, y, z, core = place()
@@ -66,19 +66,27 @@
             src_ref=src, dst_ref=dst, send_sem=ss, recv_sem=rs, device_id=to, device_id_type=MESH
         )
 
+    small = [
+        pltpu.make_async_copy(span_hbm, span_ref, in_sem.at[4]),
+        pltpu.make_async_copy(attend_hbm, attend_ref, in_sem.at[5]),
+        pltpu.make_async_copy(level_hbm, level_ref, in_sem.at[6]),
+    ]
     loads = [
         pltpu.make_async_copy(k_hbm, k_in, in_sem.at[0]),
         pltpu.make_async_copy(v_hbm, v_in, in_sem.at[1]),
         pltpu.make_async_copy(q_hbm, q_in, in_sem.at[2]),
         pltpu.make_async_copy(gate_hbm, gate, in_sem.at[3]),
     ]
-    for load in loads:
+    for load in small + loads:
         load.start()
     barrier = pltpu.get_barrier_semaphore()
     peers = [at_y(d) for d in Y_FAR] + [at_z(d) for d in Z_DIRECT] + [at_x(d) for d in X_FAR]
     peers.append(sibling)
     for peer in peers:
         pl.semaphore_signal(barrier, inc=1, device_id=peer, device_id_type=MESH)
+
+    for load in small:
+        load.wait()
 
     lane = lax.broadcasted_iota(jnp.int32, (ROWS, HD), 1)
     for i in range(NY):
@@ -119,113 +127,129 @@
         qs[0, h, 0] = q_in[:, columns(y * HPG + h, 1)]
 
     def send_kv(i):
+        unit = kv.at[0, 0, :, i]
         for d in Z_DIRECT:
-            remote(kv.at[0, 0, :, i], kv.at[0, d, :, i], z_s.at[d], z_r.at[d], at_z(d)).start()
+            got = zu_r.at[d // 4, i] if d in (2, 6) else z_r.at[d]
+            remote(unit, kv.at[0, d, :, i], z_s.at[d], got, at_z(d)).start()
+        remote(unit, kv.at[1, 0, :, i], c_s.at[0], c_r.at[0], sibling).start()
 
     def send_q(i):
         for d in X_FAR:
             remote(qs.at[0, :, i], qs.at[d, :, i], xq_s.at[d], xq_r.at[d], at_x(d)).start()
 
-    send_kv(0)
-    send_q(0)
-    for d in Y_NEAR:
+    def take_kv(d):
         unit = kv.at[0, 0, :, d]
         remote(unit, unit, ykv_s.at[d], ykv_r.at[d], sibling).wait_recv()
         send_kv(d)
-    remote(kv.at[0, 0], kv.at[1, 0], c_s.at[0], c_r.at[0], sibling).start()
-    for d in Y_NEAR:
+
+    def take_q(d):
         unit = qs.at[0, :, d]
         remote(unit, unit, yq_s.at[d], yq_r.at[d], sibling).wait_recv()
         send_q(d)
 
+    def relay(i):
+        for side, d, third, hop in ((0, 2, 3, 1), (1, 6, 5, 7)):
+            unit, half = kv.at[0, d, :, i], kv.at[0, d, side, i]
+            remote(unit, unit, z_s.at[d], zu_r.at[side, i], sibling).wait_recv()
+            remote(unit, kv.at[0, third, :, i], z_s.at[third], z_r.at[third], at_z(hop)).start()
+            remote(half, kv.at[0, 4, side, i], z4_s.at[side], z4_r.at[side], at_z(d)).start()
+            remote(unit, kv.at[1, d, :, i], c_s.at[d], c_r.at[d], sibling).start()
+
+    def share(d):
+        remote(kv.at[0, d], kv.at[1, d], c_s.at[d], c_r.at[d], sibling).start()
+
     def arrive(d):
         slot = kv.at[0, d]
         remote(slot, slot, z_s.at[d], z_r.at[d], sibling).wait_recv()
-        remote(slot, kv.at[1, d], c_s.at[d], c_r.at[d], sibling).start()
+        share(d)
 
     def from_sibling(d):
         slot = kv.at[1, d]
         remote(slot, slot, c_s.at[d], c_r.at[d], sibling).wait_recv()
 
-    def turn_values(step, parts):
+    def take_block(d):
+        block = qs.at[d]
+        remote(block, block, xq_s.at[d], xq_r.at[d], sibling).wait_recv()
+
+    def turn_values(first, parts):
         for n, (p, d) in enumerate(parts):
             vals = kv[p, d, 1].reshape(TOK, HD)
-            vt[step, :, n * TOK : (n + 1) * TOK] = vals.astype(jnp.float32).T.astype(jnp.bfloat16)
-
-    def absorb(step, parts, b, first):
+            vt[:, (first + n) * TOK : (first + n + 1) * TOK] = vals.astype(jnp.float32).T.astype(jnp.bfloat16)
+
+    def absorb(first, parts, blocks, done=lambda b: None):
         keys = jnp.concatenate([kv[p, d, 0].reshape(TOK, HD) for p, d in parts], axis=0)
         marks = jnp.concatenate([kaug[d] for _, d in parts], axis=0)
         left = jnp.concatenate([keys, marks], axis=1)
-        right = jnp.concatenate(
-            [qs[b].reshape(QR, HD), jnp.concatenate([qaug[b]] * HPG, axis=0)], axis=1
+        count = len(parts) * TOK
+        vals = jnp.concatenate(
+            [vt[:, first * TOK : first * TOK + count], jnp.ones((16, count), jnp.bfloat16)], axis=0
         )
-        scores = lax.dot_general(left, right, (((1,), (1,)), ((), ())), preferred_element_type=jnp.float32)
-        high = jnp.max(scores, axis=0, keepdims=True)
-        if not first:
-            old = top[b]
-            high = jnp.maximum(high, old)
-        probs = jnp.exp2((scores - high) * COEF).astype(jnp.bfloat16)
-        vals = jnp.concatenate([vt[step], jnp.ones((16, 2 * TOK), jnp.bfloat16)], axis=0)
-        new = jnp.dot(vals, probs, preferred_element_type=jnp.float32)
-        if first:
-            acc[b] = new
-        else:
-            acc[b] = acc[b] * jnp.exp2((old - high) * COEF) + new
-        top[b] = high
-
-    steps = [
-        ((0, 0), (1, 0)),
-        ((0, 1), (0, 7)),
-        ((1, 1), (1, 7)),
-        ((0, 2), (0, 6)),
-        ((1, 2), (1, 6)),
-        ((0, 3), (0, 5)),
-        ((1, 3), (1, 5)),
-        ((0, 4), (1, 4)),
-    ]
-
-    from_sibling(0)
-    turn_values(0, steps[0])
-    absorb(0, steps[0], 0, True)
+
+        def score(b):
+            right = jnp.concatenate(
+                [qs[b].reshape(QR, HD), jnp.concatenate([qaug[b]] * HPG, axis=0)], axis=1
+            )
+            return lax.dot_general(left, right, (((1,), (1,)), ((), ())), preferred_element_type=jnp.float32)
+
+        ahead = score(blocks[0])
+        for n, b in enumerate(blocks):
+            scores = ahead
+            if n + 1 < len(blocks):
+                ahead = score(blocks[n + 1])
+            high = jnp.max(scores, axis=0, keepdims=True)
+            if first:
+                old = top[b]
+                high = jnp.maximum(high, old)
+            probs = jnp.exp2((scores - high) * COEF).astype(jnp.bfloat16)
+            new = jnp.dot(vals, probs, preferred_element_type=jnp.float32)
+            acc[b] = acc[b] * jnp.exp2((old - high) * COEF) + new if first else new
+            top[b] = high
+            done(b)
+
+    near = [(0, 0), (1, 0), (0, 1), (0, 7), (1, 1), (1, 7), (0, 2), (0, 6), (1, 2), (1, 6)]
+    far = [(0, 3), (0, 5), (1, 3), (1, 5), (0, 4), (1, 4)]
+
+    send_kv(0)
+    send_q(0)
+    for d in (1, 7, 2, 6):
+        take_kv(d)
+    relay(0)
+    for d in (3, 5, 4):
+        take_kv(d)
+    for d in Y_NEAR:
+        take_q(d)
+    for d in Y_NEAR:
+        relay(d)
     arrive(1)
     arrive(7)
-    arrive(2)
-    arrive(6)
-    remote(kv.at[0, 2, 0], kv.at[0, 4, 0], z4_s.at[0], z4_r.at[0], at_z(2)).start()
-    remote(kv.at[0, 6, 1], kv.at[0, 4, 1], z4_s.at[1], z4_r.at[1], at_z(6)).start()
-    for d in X_FAR:
-        block = qs.at[d]
-        remote(block, block, xq_s.at[d], xq_r.at[d], sibling).wait_recv()
-    for b in (1, 2, 3):
-        absorb(0, steps[0], b, True)
+    for d in (0, 2, 6, 1, 7):
+        from_sibling(d)
+    turn_values(0, near)
+    absorb(0, near, [0])
+    take_block(1)
+    take_block(3)
+    absorb(0, near, [1, 3])
     arrive(3)
     arrive(5)
-    for step in (1, 2, 3, 4):
-        if step in (2, 4):
-            for _, d in steps[step]:
-                from_sibling(d)
-        turn_values(step, steps[step])
-        for b in range(NX):
-            absorb(step, steps[step], b, False)
-        if step == 2:
-            for half in (0, 1):
-                slot = kv.at[0, 4, half]
-                remote(slot, slot, z4_s.at[half], z4_r.at[half], sibling).wait_recv()
-            remote(kv.at[0, 4], kv.at[1, 4], c_s.at[4], c_r.at[4], sibling).start()
-    from_sibling(3)
-    from_sibling(5)
-    from_sibling(4)
-    for step in (5, 6, 7):
-        turn_values(step, steps[step])
-    for b in (2, 1, 3, 0):
-        for step in (5, 6, 7):
-            absorb(step, steps[step], b, False)
+    take_block(2)
+    absorb(0, near, [2])
+    for half in (0, 1):
+        slot = kv.at[0, 4, half]
+        remote(slot, slot, z4_s.at[half], z4_r.at[half], sibling).wait_recv()
+    share(4)
+    for d in (3, 5, 4):
+        from_sibling(d)
+    turn_values(len(near), far)
+
+    def give(b):
         if b:
             o_send[b] = (acc[b, 0:HD, :] / acc[b, HD : HD + 1, :]).astype(jnp.bfloat16)
             s_send[b] = jnp.concatenate([top[b], acc[b, HD : HD + 7, :]], axis=0)
             to = at_x(-b)
             remote(o_send.at[b], o_recv.at[b], xo_s.at[b], xo_r.at[b], to).start()
             remote(s_send.at[b], s_recv.at[b], xs_s.at[b], xs_r.at[b], to).start()
+
+    absorb(len(near), far, [2, 1, 3, 0], give)
 
     for b in (1, 2, 3):
         part, stat = o_recv.at[b], s_recv.at[b]
@@ -260,7 +284,7 @@
         remote(kv.at[0, 0, :, d], kv.at[0, 0, :, d], ykv_s.at[d], ykv_r.at[d], sibling).wait_send()
         remote(qs.at[0, :, d], qs.at[0, :, d], yq_s.at[d], yq_r.at[d], sibling).wait_send()
         remote(attn_send.at[d], attn_send.at[d], yo_s.at[d], yo_r.at[d], sibling).wait_send()
-    for d in Z_DIRECT:
+    for d in Z_DIRECT + (3, 5):
         remote(kv.at[0, 0], kv.at[0, 0], z_s.at[d], z_r.at[d], sibling).wait_send()
     for half in (0, 1):
         remote(kv.at[0, 4, half], kv.at[0, 4, half], z4_s.at[half], z4_r.at[half], sibling).wait_send()
@@ -275,23 +299,25 @@
 def local(queries, key_rows, value_rows, block_span, attend, noise_level, gate_table):
     bf16, f32 = jnp.bfloat16, jnp.float32
     dma = pltpu.SemaphoreType.DMA
-    anywhere = pl.BlockSpec(memory_space=pl.ANY)
-    smem = pl.BlockSpec(memory_space=pltpu.SMEM)
+    hbm = pl.BlockSpec(memory_space=pltpu.HBM)
     return pl.pallas_call(
         kernel,
         out_shape=jax.ShapeDtypeStruct(queries.shape, bf16),
-        in_specs=[anywhere, anywhere, anywhere, smem, smem, smem, anywhere],
+        in_specs=[hbm] * 7,
         out_specs=pl.BlockSpec(memory_space=pltpu.VMEM),
         scratch_shapes=[
             pltpu.VMEM(queries.shape, bf16),
             pltpu.VMEM(key_rows.shape, bf16),
             pltpu.VMEM(value_rows.shape, bf16),
             pltpu.VMEM(gate_table.shape, f32),
+            pltpu.SMEM(block_span.shape, jnp.int32),
+            pltpu.SMEM(attend.shape, jnp.int32),
+            pltpu.SMEM(noise_level.shape, jnp.int32),
             pltpu.VMEM((2, NZ, 2, NY, ROWS, HD), bf16),
             pltpu.VMEM((NX, HPG, NY, ROWS, HD), bf16),
             pltpu.VMEM((NZ, TOK, HD), bf16),
             pltpu.VMEM((NX, TOK, HD), bf16),
-            pltpu.VMEM((8, HD, 2 * TOK), bf16),
+            pltpu.VMEM((HD, 2 * NZ * TOK), bf16),
             pltpu.VMEM((NX, HD + 16, QR), f32),
             pltpu.VMEM((NX, 1, QR), f32),
             pltpu.VMEM((NX, HD, QR), bf16),
@@ -300,15 +326,15 @@
             pltpu.VMEM((NX, 8, QR), f32),
             pltpu.VMEM((NY, ROWS, HPG * HD), bf16),
             pltpu.VMEM((NY, ROWS, HPG * HD), bf16),
-            dma((4,)),
+            dma((7,)),
             dma((8,)), dma((8,)), dma((8,)), dma((8,)),
-            dma((8,)), dma((8,)), dma((2,)), dma((2,)),
+            dma((8,)), dma((8,)), dma((2, 8)), dma((2,)), dma((2,)),
             dma((8,)), dma((8,)),
             dma((4,)), dma((4,)), dma((4,)), dma((4,)), dma((4,)), dma((4,)),
             dma((8,)), dma((8,)),
         ],
         compiler_params=pltpu.CompilerParams(
-            collective_id=0, has_side_effects=True, vmem_limit_bytes=48 << 20
+            collective_id=0, has_side_effects=True, vmem_limit_bytes=63 << 20
         ),
     )(queries, key_rows, value_rows, block_span, attend, noise_level, gate_table)
 

time: 54.5 us -> 46.7 us (0.86)
  local copies, waits for them, and re-layouts: 6.04 us -> 1.54 us
  Pallas kernels: 47.9 us -> 45 us
    unnamed x15 -> x1, local copies, waits for them, and re-layouts: 6.04 us -> 1.54 us
    pallas_call x1, Pallas kernels: 47.9 us -> 45 us  [local(): pl.pallas_call(kernel, out_shape=jax.ShapeDtypeStruct(queries.shape, bf16...]
where the time goes in v2:
time: 46.7 us; the launch traced here: 46.6 us
  Pallas kernels  45 us (96%)
  local copies, waits for them, and re-layouts  1.54 us (3%)
    pallas_call x1, Pallas kernels, local(): pl.pallas_call(kernel, out_shape=jax.ShapeDtypeStruct(queries.shape, bf16...  45 us
    unnamed x1, local copies, waits for them, and re-layouts  1.54 us

profile of v2, /device:TPU:1, one launch (start us, length us, event | category | flops | bytes accessed | tf_op | source)
XLA Modules:
  0.0 46.6 jit_solution(17342023780322123072)
XLA Ops:
  0.0 45.0 %shard_map.73 = bf16[16,3072]{1,0:T(8,128)(2,1)} custom-call(bf16[16,3072]{1,0:T(8,128)(2,1)} %q_hbm.1, bf16[16,1024]{1,0:T(8,128)(2,1)} %k_hbm.1, bf16[16,1024]{1,0:T(8,128)(2,1)} %v_hbm.1, s32[128]{0:T(128)} %span_hbm.1, s32[4,4]{1,0:T(4,128)} %attend_hbm.1, s32[4]{0:T(128)} %level_hbm.1, f32[32,3072]{1,0:T(8,128)} %gate_hbm.1), custom_call_target="tpu_custom_call" | custom-call | tf_op jit(solution)/shard_map/pallas_call | solution.py:303
  45.0 1.5 %copy.9 = bf16[16,3072]{1,0:T(8,128)(2,1)} copy(bf16[16,3072]{1,0:T(8,128)(2,1)} %shard_map.73) | data formatting | bytes 196608

commit v3 on v2

--- a/solution.py
+++ b/solution.py
@@ -43,9 +43,9 @@
 
 
 def kernel(
-    q_hbm, k_hbm, v_hbm, span_hbm, attend_hbm, level_hbm, gate_hbm, out_ref,
-    q_in, k_in, v_in, gate, span_ref, attend_ref, level_ref, kv, qs, kaug, qaug, vt, acc, top, o_send, s_send, o_recv, s_recv,
-    attn_send, attn, in_sem, ykv_s, ykv_r, yq_s, yq_r, z_s, z_r, zu_r, z4_s, z4_r, c_s, c_r, xq_s, xq_r,
+    q_hbm, k_hbm, v_hbm, span_hbm, attend_hbm, level_hbm, gate_hbm, out_hbm,
+    q_in, k_in, v_in, gate, span_ref, attend_ref, level_ref, kv, qs, kaug, qaug, acc, top, o_send, s_send, o_recv, s_recv,
+    attn_send, attn, out_ref, in_sem, out_sem, ykv_s, ykv_r, yq_s, yq_r, z_s, z_r, zu_r, z4_s, z4_r, c_s, c_r, xq_s, xq_r,
     xo_s, xo_r, xs_s, xs_r, yo_s, yo_r,
 ):
     x, y, z, core = place()
@@ -102,7 +102,7 @@
                 bias = jnp.where(lane == s, low, bias)
             qaug[j, i * ROWS : (i + 1) * ROWS, :] = bias.astype(jnp.bfloat16)
 
-    for load in loads:
+    for load in loads[:3]:
         load.wait()
     pl.semaphore_wait(barrier, len(peers))
 
@@ -128,9 +128,8 @@
 
     def send_kv(i):
         unit = kv.at[0, 0, :, i]
-        for d in Z_DIRECT:
-            got = zu_r.at[d // 4, i] if d in (2, 6) else z_r.at[d]
-            remote(unit, kv.at[0, d, :, i], z_s.at[d], got, at_z(d)).start()
+        for side, d in ((0, 2), (1, 6)):
+            remote(unit, kv.at[0, d, :, i], z_s.at[d], zu_r.at[side, i], at_z(d)).start()
         remote(unit, kv.at[1, 0, :, i], c_s.at[0], c_r.at[0], sibling).start()
 
     def send_q(i):
@@ -151,8 +150,8 @@
         for side, d, third, hop in ((0, 2, 3, 1), (1, 6, 5, 7)):
             unit, half = kv.at[0, d, :, i], kv.at[0, d, side, i]
             remote(unit, unit, z_s.at[d], zu_r.at[side, i], sibling).wait_recv()
+            remote(half, kv.at[0, 4, side, i], z4_s.at[side], z4_r.at[side], at_z(d)).start()
             remote(unit, kv.at[0, third, :, i], z_s.at[third], z_r.at[third], at_z(hop)).start()
-            remote(half, kv.at[0, 4, side, i], z4_s.at[side], z4_r.at[side], at_z(d)).start()
             remote(unit, kv.at[1, d, :, i], c_s.at[d], c_r.at[d], sibling).start()
 
     def share(d):
@@ -171,106 +170,138 @@
         block = qs.at[d]
         remote(block, block, xq_s.at[d], xq_r.at[d], sibling).wait_recv()
 
-    def turn_values(first, parts):
-        for n, (p, d) in enumerate(parts):
-            vals = kv[p, d, 1].reshape(TOK, HD)
-            vt[:, (first + n) * TOK : (first + n + 1) * TOK] = vals.astype(jnp.float32).T.astype(jnp.bfloat16)
-
-    def absorb(first, parts, blocks, done=lambda b: None):
+    def absorb(first, parts, groups, done=lambda b: None):
         keys = jnp.concatenate([kv[p, d, 0].reshape(TOK, HD) for p, d in parts], axis=0)
         marks = jnp.concatenate([kaug[d] for _, d in parts], axis=0)
-        left = jnp.concatenate([keys, marks], axis=1)
-        count = len(parts) * TOK
-        vals = jnp.concatenate(
-            [vt[:, first * TOK : first * TOK + count], jnp.ones((16, count), jnp.bfloat16)], axis=0
-        )
-
-        def score(b):
-            right = jnp.concatenate(
-                [qs[b].reshape(QR, HD), jnp.concatenate([qaug[b]] * HPG, axis=0)], axis=1
+        right = jnp.concatenate([keys, marks], axis=1)
+        vals = jnp.concatenate([kv[p, d, 1].reshape(TOK, HD) for p, d in parts], axis=0)
+        vals = jnp.concatenate([vals, jnp.ones(vals.shape, jnp.bfloat16)], axis=1)
+
+        def score(group):
+            left = jnp.concatenate(
+                [
+                    jnp.concatenate(
+                        [qs[b].reshape(QR, HD), jnp.concatenate([qaug[b]] * HPG, axis=0)], axis=1
+                    )
+                    for b in group
+                ],
+                axis=0,
             )
             return lax.dot_general(left, right, (((1,), (1,)), ((), ())), preferred_element_type=jnp.float32)
 
-        ahead = score(blocks[0])
-        for n, b in enumerate(blocks):
+        ahead = score(groups[0])
+        for n, group in enumerate(groups):
             scores = ahead
-            if n + 1 < len(blocks):
-                ahead = score(blocks[n + 1])
-            high = jnp.max(scores, axis=0, keepdims=True)
+            if n + 1 < len(groups) and True:
+                ahead = score(groups[n + 1])
+            high = jnp.max(scores, axis=1, keepdims=True)
             if first:
-                old = top[b]
+                old = jnp.concatenate([top[b][:, 0:1] for b in group], axis=0)
                 high = jnp.maximum(high, old)
             probs = jnp.exp2((scores - high) * COEF).astype(jnp.bfloat16)
-            new = jnp.dot(vals, probs, preferred_element_type=jnp.float32)
-            acc[b] = acc[b] * jnp.exp2((old - high) * COEF) + new if first else new
-            top[b] = high
-            done(b)
-
-    near = [(0, 0), (1, 0), (0, 1), (0, 7), (1, 1), (1, 7), (0, 2), (0, 6), (1, 2), (1, 6)]
-    far = [(0, 3), (0, 5), (1, 3), (1, 5), (0, 4), (1, 4)]
+            new = jnp.dot(probs, vals, preferred_element_type=jnp.float32)
+            if first:
+                shrink = jnp.exp2((old - high) * COEF)
+            for k, b in enumerate(group):
+                rows = slice(k * QR, (k + 1) * QR)
+                acc[b] = acc[b] * shrink[rows] + new[rows] if first else new[rows]
+                top[b] = jnp.broadcast_to(high[rows], (QR, HD))
+                done(b)
+            if n + 1 < len(groups) and not True:
+                ahead = score(groups[n + 1])
+
+    near = [(0, 0), (1, 0), (0, 2), (0, 6), (1, 2), (1, 6)]
+    far = [(0, 1), (0, 7), (1, 1), (1, 7), (0, 3), (0, 5), (1, 3), (1, 5), (0, 4), (1, 4)]
 
     send_kv(0)
     send_q(0)
     for d in (1, 7, 2, 6):
         take_kv(d)
-    relay(0)
     for d in (3, 5, 4):
         take_kv(d)
+    for d in (1, 7):
+        remote(kv.at[0, 0], kv.at[0, d], z_s.at[d], z_r.at[d], at_z(d)).start()
     for d in Y_NEAR:
         take_q(d)
-    for d in Y_NEAR:
+    for d in (0,) + Y_NEAR:
         relay(d)
     arrive(1)
     arrive(7)
-    for d in (0, 2, 6, 1, 7):
+    for d in (0, 2, 6):
         from_sibling(d)
-    turn_values(0, near)
-    absorb(0, near, [0])
     take_block(1)
     take_block(3)
-    absorb(0, near, [1, 3])
+    take_block(2)
+    absorb(0, near, [[2], [1]])
     arrive(3)
     arrive(5)
-    take_block(2)
-    absorb(0, near, [2])
     for half in (0, 1):
         slot = kv.at[0, 4, half]
         remote(slot, slot, z4_s.at[half], z4_r.at[half], sibling).wait_recv()
-    share(4)
-    for d in (3, 5, 4):
+        remote(slot, kv.at[1, 4, half], c_s.at[4], c_r.at[4], sibling).start()
+    for d in (1, 7, 3, 5, 4):
         from_sibling(d)
-    turn_values(len(near), far)
+
+    lanes = lax.broadcasted_iota(jnp.int32, (TOK, HD), 1)
+
+    def stats_of(b):
+        stats = jnp.zeros((TOK, HD), jnp.float32)
+        for h in range(HPG):
+            rows = slice(h * TOK, (h + 1) * TOK)
+            stats = jnp.where(lanes == h, top[b, rows, :], stats)
+            stats = jnp.where(lanes == HPG + h, acc[b, rows, HD : 2 * HD], stats)
+        return stats.T[0:8, :]
 
     def give(b):
+        s_send[b] = stats_of(b)
         if b:
-            o_send[b] = (acc[b, 0:HD, :] / acc[b, HD : HD + 1, :]).astype(jnp.bfloat16)
-            s_send[b] = jnp.concatenate([top[b], acc[b, HD : HD + 7, :]], axis=0)
+            mean = (acc[b, :, 0:HD] / acc[b, :, HD : 2 * HD]).astype(jnp.bfloat16)
+            o_send[b] = mean.reshape(HPG, NY, ROWS, HD)
             to = at_x(-b)
-            remote(o_send.at[b], o_recv.at[b], xo_s.at[b], xo_r.at[b], to).start()
             remote(s_send.at[b], s_recv.at[b], xs_s.at[b], xs_r.at[b], to).start()
-
-    absorb(len(near), far, [2, 1, 3, 0], give)
+            for part, lo, hi in ((0, 3, 6), (1, 0, 3), (1, 6, 8)):
+                remote(
+                    o_send.at[b, :, lo:hi], o_recv.at[b, :, lo:hi], xo_s.at[part, b], xo_r.at[part, b], to
+                ).start()
+
+    absorb(1, far, [[2], [1]], give)
+    absorb(0, near + far, [[3], [0]], give)
 
     for b in (1, 2, 3):
-        part, stat = o_recv.at[b], s_recv.at[b]
-        remote(stat, stat, xs_s.at[b], xs_r.at[b], sibling).wait_recv()
-        remote(part, part, xo_s.at[b], xo_r.at[b], sibling).wait_recv()
-    tops = [top[0]] + [s_recv[b, 0:1, :] for b in (1, 2, 3)]
+        note = s_recv.at[b]
+        remote(note, note, xs_s.at[b], xs_r.at[b], sibling).wait_recv()
+    notes = [s_send[0]] + [s_recv[b] for b in (1, 2, 3)]
+    tops = [note[0:HPG] for note in notes]
     highest = functools.reduce(jnp.maximum, tops)
-    scales = [jnp.exp2((t - highest) * COEF) for t in tops]
-    sums = [acc[0, HD : HD + 1, :]] + [s_recv[b, 1:2, :] for b in (1, 2, 3)]
-    shares = [scale * total for scale, total in zip(scales, sums)]
+    shares = [note[HPG : 2 * HPG] * jnp.exp2((t - highest) * COEF) for note, t in zip(notes, tops)]
     whole = 1.0 / functools.reduce(jnp.add, shares)
-    merged = acc[0, 0:HD, :] * (scales[0] * whole)
+    shares = [share_ * whole for share_ in shares]
+    shares = jnp.concatenate(shares + [jnp.zeros((TOK - NX * HPG, TOK), jnp.float32)], axis=0).T
+
+    def merge(lo, hi):
+        rows = slice(lo * ROWS, hi * ROWS)
+        for h in range(HPG):
+            own = slice(h * TOK + lo * ROWS, h * TOK + hi * ROWS)
+            total = acc[0, own, 0:HD] / acc[0, own, HD : 2 * HD] * shares[rows, h : h + 1]
+            for b in (1, 2, 3):
+                part = o_recv[b, h, lo:hi].reshape((hi - lo) * ROWS, HD).astype(jnp.float32)
+                total = total + part * shares[rows, b * HPG + h : b * HPG + h + 1]
+            total = total.astype(jnp.bfloat16).reshape(hi - lo, ROWS, HD)
+            attn_send[lo:hi, :, h * HD : (h + 1) * HD] = total
+        for d in range(max(lo, 1), hi):
+            remote(attn_send.at[d], attn.at[y], yo_s.at[d], yo_r.at[d], at_y(-d)).start()
+
     for b in (1, 2, 3):
-        merged = merged + o_recv[b].astype(jnp.float32) * (shares[b] * whole)
-    for h in range(HPG):
-        rows = merged[:, h * TOK : (h + 1) * TOK].T.astype(jnp.bfloat16)
-        for i in range(NY):
-            attn_send[i, :, h * HD : (h + 1) * HD] = rows[i * ROWS : (i + 1) * ROWS, :]
-    for d in Y_FAR:
-        remote(attn_send.at[d], attn.at[y], yo_s.at[d], yo_r.at[d], at_y(-d)).start()
+        part = o_recv.at[b, :, 3:6]
+        remote(part, part, xo_s.at[0, b], xo_r.at[0, b], sibling).wait_recv()
+    merge(3, 6)
+    for b in (1, 2, 3):
+        part = o_recv.at[b, :, 0:5]
+        remote(part, part, xo_s.at[1, b], xo_r.at[1, b], sibling).wait_recv()
+    merge(6, 8)
+    merge(0, 3)
     attn[y] = attn_send[0]
+    loads[3].wait()
     level = level_ref[span_ref[block_of(x, y, z)]]
     gates = gate[pl.ds(level, 1), :]
     for d in Y_NEAR:
@@ -279,6 +310,9 @@
     for g in range(NY):
         cols = slice(g * HPG * HD, (g + 1) * HPG * HD)
         out_ref[:, cols] = (gates[:, cols] * attn[g].astype(jnp.float32)).astype(jnp.bfloat16)
+
+    result = pltpu.make_async_copy(out_ref, out_hbm, out_sem)
+    result.start()
 
     for d in Y_NEAR:
         remote(kv.at[0, 0, :, d], kv.at[0, 0, :, d], ykv_s.at[d], ykv_r.at[d], sibling).wait_send()
@@ -292,8 +326,10 @@
         remote(kv.at[0, d], kv.at[0, d], c_s.at[d], c_r.at[d], sibling).wait_send()
     for d in X_FAR:
         remote(qs.at[0], qs.at[0], xq_s.at[d], xq_r.at[d], sibling).wait_send()
-        remote(o_send.at[d], o_send.at[d], xo_s.at[d], xo_r.at[d], sibling).wait_send()
+        remote(o_send.at[d, :, 3:6], o_send.at[d, :, 3:6], xo_s.at[0, d], xo_r.at[0, d], sibling).wait_send()
+        remote(o_send.at[d, :, 0:5], o_send.at[d, :, 0:5], xo_s.at[1, d], xo_r.at[1, d], sibling).wait_send()
         remote(s_send.at[d], s_send.at[d], xs_s.at[d], xs_r.at[d], sibling).wait_send()
+    result.wait()
 
 
 def local(queries, key_rows, value_rows, block_span, attend, noise_level, gate_table):
@@ -304,7 +340,7 @@
         kernel,
         out_shape=jax.ShapeDtypeStruct(queries.shape, bf16),
         in_specs=[hbm] * 7,
-        out_specs=pl.BlockSpec(memory_space=pltpu.VMEM),
+        out_specs=hbm,
         scratch_shapes=[
             pltpu.VMEM(queries.shape, bf16),
             pltpu.VMEM(key_rows.shape, bf16),
@@ -317,20 +353,21 @@
             pltpu.VMEM((NX, HPG, NY, ROWS, HD), bf16),
             pltpu.VMEM((NZ, TOK, HD), bf16),
             pltpu.VMEM((NX, TOK, HD), bf16),
-            pltpu.VMEM((HD, 2 * NZ * TOK), bf16),
-            pltpu.VMEM((NX, HD + 16, QR), f32),
-            pltpu.VMEM((NX, 1, QR), f32),
-            pltpu.VMEM((NX, HD, QR), bf16),
-            pltpu.VMEM((NX, 8, QR), f32),
-            pltpu.VMEM((NX, HD, QR), bf16),
-            pltpu.VMEM((NX, 8, QR), f32),
+            pltpu.VMEM((NX, QR, 2 * HD), f32),
+            pltpu.VMEM((NX, QR, HD), f32),
+            pltpu.VMEM((NX, HPG, NY, ROWS, HD), bf16),
+            pltpu.VMEM((NX, 8, TOK), f32),
+            pltpu.VMEM((NX, HPG, NY, ROWS, HD), bf16),
+            pltpu.VMEM((NX, 8, TOK), f32),
             pltpu.VMEM((NY, ROWS, HPG * HD), bf16),
             pltpu.VMEM((NY, ROWS, HPG * HD), bf16),
+            pltpu.VMEM(queries.shape, bf16),
             dma((7,)),
+            dma,
             dma((8,)), dma((8,)), dma((8,)), dma((8,)),
             dma((8,)), dma((8,)), dma((2, 8)), dma((2,)), dma((2,)),
             dma((8,)), dma((8,)),
-            dma((4,)), dma((4,)), dma((4,)), dma((4,)), dma((4,)), dma((4,)),
+            dma((4,)), dma((4,)), dma((2, 4)), dma((2, 4)), dma((4,)), dma((4,)),
             dma((8,)), dma((8,)),
         ],
         compiler_params=pltpu.CompilerParams(

time: 46.7 us -> 45.2 us (0.968)
  Pallas kernels: 45 us -> 43.5 us
    pallas_call x1, Pallas kernels: 45 us -> 43.5 us  [local(): pl.pallas_call(kernel, out_shape=jax.ShapeDtypeStruct(queries.shape, bf16...]
where the time goes in v3:
time: 45.2 us; the launch traced here: 45 us
  Pallas kernels  43.5 us (96%)
  local copies, waits for them, and re-layouts  1.54 us (3%)
    pallas_call x1, Pallas kernels, local(): pl.pallas_call(kernel, out_shape=jax.ShapeDtypeStruct(queries.shape, bf16...  43.5 us
    unnamed x1, local copies, waits for them, and re-layouts  1.54 us

profile of v3, /device:TPU:1, one launch (start us, length us, event | category | flops | bytes accessed | tf_op | source)
XLA Modules:
  0.0 45.0 jit_solution(11159440884894172148)
XLA Ops:
  0.0 43.5 %shard_map.73 = bf16[16,3072]{1,0:T(8,128)(2,1)} custom-call(bf16[16,3072]{1,0:T(8,128)(2,1)} %q_hbm.1, bf16[16,1024]{1,0:T(8,128)(2,1)} %k_hbm.1, bf16[16,1024]{1,0:T(8,128)(2,1)} %v_hbm.1, s32[128]{0:T(128)} %span_hbm.1, s32[4,4]{1,0:T(4,128)} %attend_hbm.1, s32[4]{0:T(128)} %level_hbm.1, f32[32,3072]{1,0:T(8,128)} %gate_hbm.1), custom_call_target="tpu_custom_call" | custom-call | tf_op jit(solution)/shard_map/pallas_call | solution.py:339
  43.5 1.5 %copy.9 = bf16[16,3072]{1,0:T(8,128)(2,1)} copy(bf16[16,3072]{1,0:T(8,128)(2,1)} %shard_map.73) | data formatting | bytes 196608

commit v4 on v3

--- a/solution.py
+++ b/solution.py
@@ -221,17 +221,17 @@
         take_kv(d)
     for d in (1, 7):
         remote(kv.at[0, 0], kv.at[0, d], z_s.at[d], z_r.at[d], at_z(d)).start()
+    relay(0)
     for d in Y_NEAR:
         take_q(d)
-    for d in (0,) + Y_NEAR:
+    for d in Y_NEAR:
         relay(d)
     arrive(1)
     arrive(7)
     for d in (0, 2, 6):
         from_sibling(d)
+    take_block(2)
     take_block(1)
-    take_block(3)
-    take_block(2)
     absorb(0, near, [[2], [1]])
     arrive(3)
     arrive(5)
@@ -265,6 +265,7 @@
                 ).start()
 
     absorb(1, far, [[2], [1]], give)
+    take_block(3)
     absorb(0, near + far, [[3], [0]], give)
 
     for b in (1, 2, 3):

time: 45.2 us -> 45 us (level)
  no operation moved by 1% of the time
where the time goes in v4:
time: 45 us; the launch traced here: 44.8 us
  Pallas kernels  43.3 us (96%)
  local copies, waits for them, and re-layouts  1.54 us (3%)
    pallas_call x1, Pallas kernels, local(): pl.pallas_call(kernel, out_shape=jax.ShapeDtypeStruct(queries.shape, bf16...  43.3 us
    unnamed x1, local copies, waits for them, and re-layouts  1.54 us

profile of v4, /device:TPU:1, one launch (start us, length us, event | category | flops | bytes accessed | tf_op | source)
XLA Modules:
  0.0 44.8 jit_solution(7840105820359454058)
XLA Ops:
  0.0 43.3 %shard_map.73 = bf16[16,3072]{1,0:T(8,128)(2,1)} custom-call(bf16[16,3072]{1,0:T(8,128)(2,1)} %q_hbm.1, bf16[16,1024]{1,0:T(8,128)(2,1)} %k_hbm.1, bf16[16,1024]{1,0:T(8,128)(2,1)} %v_hbm.1, s32[128]{0:T(128)} %span_hbm.1, s32[4,4]{1,0:T(4,128)} %attend_hbm.1, s32[4]{0:T(128)} %level_hbm.1, f32[32,3072]{1,0:T(8,128)} %gate_hbm.1), custom_call_target="tpu_custom_call" | custom-call | tf_op jit(solution)/shard_map/pallas_call | solution.py:340
  43.3 1.5 %copy.9 = bf16[16,3072]{1,0:T(8,128)(2,1)} copy(bf16[16,3072]{1,0:T(8,128)(2,1)} %shard_map.73) | data formatting | bytes 196608
